TPU v7x, 32 devices: a whole 2x2x4 slice. The times are simulated.
32 devices in a mesh: rep: 2 (over core), fsdp: 16 (over z, y, x).
Axes of the slice: x: 2, y: 2, z: 4, core: 2. Of those that a mesh axis runs over, the one named last changes fastest.
Arguments:
- hidden: bfloat16 [24576, 768], P(('rep', 'fsdp')), may hold values from -6 to 6
- qry_len: int32 [64], P(('rep', 'fsdp')), may hold values from 103 to 128, as said below
- psg_len: int32 [32], P(('rep', 'fsdp')), may hold values from 410 to 512, as said below
- qry_grad: float32 [64, 768], P(('rep', 'fsdp')), may hold values from -192 to 192
- psg_grad: float32 [32, 768], P(('rep', 'fsdp')), may hold values from -192 to 192
- w_qkv: bfloat16 [2, 768, 2304], P(None, 'fsdp'), may hold values from -0.21875 to 0.21875
- w_o: bfloat16 [2, 768, 768], P(None, 'fsdp'), may hold values from -0.625 to 0.625
- w_in: bfloat16 [2, 768, 3072], P(None, 'fsdp'), may hold values from -0.21875 to 0.21875
- w_out: bfloat16 [2, 3072, 768], P(None, 'fsdp'), may hold values from -0.109375 to 0.109375
- biases: bfloat16 [2, 6, 768], P(None, None, 'fsdp'), may hold values from -1.75 to 1.75
- gains: bfloat16 [2, 2, 768], P(None, None, 'fsdp'), may hold values from 0.25 to 1.75
- in_bias: bfloat16 [2, 3072], P(None, 'fsdp'), may hold values from -1.75 to 1.75
Outputs:
- mixed: bfloat16 [24576, 768], P(('rep', 'fsdp'))
- grad_hidden: bfloat16 [24576, 768], P(('rep', 'fsdp'))
- grad_qkv: float32 [2, 768, 2304], P(None, 'fsdp')
- grad_o: float32 [2, 768, 768], P(None, 'fsdp')
- grad_in: float32 [2, 768, 3072], P(None, 'fsdp')
- grad_out: float32 [2, 3072, 768], P(None, 'fsdp')
- grad_biases: float32 [2, 6, 768], P(None, None, 'fsdp')
- grad_gains: float32 [2, 2, 768], P(None, None, 'fsdp')
- grad_in_bias: float32 [2, 3072], P(None, 'fsdp')
Inputs may be any that keep to these rules, and one draw needn't show every extreme that they name: `qry_len`: each query has 103 to 128 live slots; some query has all 128. `psg_len`: each passage has 410 to 512 live slots; some passage has all 512.
All inputs are finite; a program needn't handle non-finite values.
Results may differ from a plain program's by a relative error of at most 0.017.
Values may be sent and summed in bfloat16 or wider, within the bound.
A program may use at most 320 MiB of HBM per device.

v0:
```python
import jax
import jax.numpy as jnp
from jax import lax
from jax.sharding import PartitionSpec as P

H = 12
HD = 64
SHORT = 128
LONG = 512


NORM_EPS = 1e-12
MASKED = -1e30


def norm_rows(resid, gain, shift):
    average = jnp.mean(resid, axis=-1, keepdims=True)
    centered = resid - average
    spread = jnp.mean(centered * centered, axis=-1, keepdims=True)
    return centered * lax.rsqrt(spread + NORM_EPS) * gain + shift


def gelu_exact(values):
    return jax.nn.gelu(values, approximate=False)


def split_kinds(rows, short_count):
    cut = short_count * SHORT
    short_part = rows[:cut].reshape((short_count, SHORT) + rows.shape[1:])
    long_part = rows[cut:].reshape((-1, LONG) + rows.shape[1:])
    return (short_part, long_part)


def join_kinds(short_part, long_part):
    short_flat = short_part.reshape((-1,) + short_part.shape[2:])
    long_flat = long_part.reshape((-1,) + long_part.shape[2:])
    return jnp.concatenate([short_flat, long_flat], axis=0)


def fetch_layer(w_qkv, w_o, w_in, w_out, biases, gains, in_bias, which_layer):
    bias_rows = in_bias[which_layer].reshape(1, -1)
    complete = (
        lax.all_gather(w_qkv[which_layer], "fsdp", axis=0, tiled=True),
        lax.all_gather(w_o[which_layer], "fsdp", axis=0, tiled=True),
        lax.all_gather(w_in[which_layer], "fsdp", axis=0, tiled=True),
        lax.all_gather(w_out[which_layer], "fsdp", axis=0, tiled=True),
        lax.all_gather(biases[which_layer], "fsdp", axis=1, tiled=True),
        lax.all_gather(gains[which_layer], "fsdp", axis=1, tiled=True),
        lax.all_gather(bias_rows, "fsdp", axis=0, tiled=True),
    )
    return (
        complete[0],
        complete[1],
        complete[2],
        complete[3],
        complete[4],
        complete[5],
        complete[6].reshape(-1),
    )


def attend_kind(packed, lengths):
    query_rows = packed[:, :, 0]
    key_rows = packed[:, :, 1]
    value_rows = packed[:, :, 2]
    score_scale = query_rows.shape[-1] ** (-0.5)
    scores = (
        jnp.einsum("bqhd,bkhd->bhqk", query_rows, key_rows, preferred_element_type=jnp.float32)
        * score_scale
    )
    visible = jnp.arange(key_rows.shape[1])[None, :] < lengths[:, None]
    scores = jnp.where(visible[:, None, None, :], scores, MASKED)
    highest = jnp.max(scores, axis=-1, keepdims=True)
    exponentials = jnp.exp(scores - highest)
    probabilities = exponentials / jnp.sum(exponentials, axis=-1, keepdims=True)
    context = jnp.einsum(
        "bhqk,bkhd->bqhd",
        probabilities.astype(jnp.bfloat16),
        value_rows,
        preferred_element_type=jnp.float32,
    )
    return (context, probabilities)


def attend_back(packed, probabilities, d_context):
    query_rows = packed[:, :, 0]
    key_rows = packed[:, :, 1]
    value_rows = packed[:, :, 2]
    score_scale = query_rows.shape[-1] ** (-0.5)
    d_probs = jnp.einsum(
        "bqhd,bkhd->bhqk", d_context, value_rows, preferred_element_type=jnp.float32
    )
    d_values = jnp.einsum(
        "bhqk,bqhd->bkhd",
        probabilities.astype(jnp.bfloat16),
        d_context,
        preferred_element_type=jnp.float32,
    )
    inner = jnp.sum(d_probs * probabilities, axis=-1, keepdims=True)
    d_scores = (probabilities * (d_probs - inner)).astype(jnp.bfloat16)
    d_queries = (
        jnp.einsum("bhqk,bkhd->bqhd", d_scores, key_rows, preferred_element_type=jnp.float32)
        * score_scale
    )
    d_keys = (
        jnp.einsum("bhqk,bqhd->bkhd", d_scores, query_rows, preferred_element_type=jnp.float32)
        * score_scale
    )
    return jnp.stack([d_queries, d_keys, d_values], axis=2)


def layer_forward(inputs, weights, qry_len, psg_len):
    w_qkv, w_o, w_in, w_out, bias_rows, gain_rows, in_bias = weights
    bias_float = bias_rows.astype(jnp.float32)
    gain_float = gain_rows.astype(jnp.float32)
    row_count = inputs.shape[0]
    inputs_low = inputs.astype(jnp.bfloat16)
    qkv_bias = jnp.concatenate([bias_float[0], jnp.zeros_like(bias_float[0]), bias_float[1]])
    packed = (jnp.dot(inputs_low, w_qkv, preferred_element_type=jnp.float32) + qkv_bias).astype(
        jnp.bfloat16
    )
    packed = packed.reshape(row_count, 3, H, HD)
    short_pack, long_pack = split_kinds(packed, qry_len.shape[0])
    short_context, short_softmax = attend_kind(short_pack, qry_len)
    long_context, long_softmax = attend_kind(long_pack, psg_len)
    context = join_kinds(short_context, long_context).reshape(row_count, -1).astype(jnp.bfloat16)
    attended = jnp.dot(context, w_o, preferred_element_type=jnp.float32) + bias_float[2]
    first_resid = inputs + attended
    first_norm = norm_rows(first_resid, gain_float[0], bias_float[3])
    first_low = first_norm.astype(jnp.bfloat16)
    upward = jnp.dot(first_low, w_in, preferred_element_type=jnp.float32) + in_bias.astype(
        jnp.float32
    )
    active_low = gelu_exact(upward).astype(jnp.bfloat16)
    second_resid = first_norm + (
        jnp.dot(active_low, w_out, preferred_element_type=jnp.float32) + bias_float[4]
    )
    outputs = norm_rows(second_resid, gain_float[1], bias_float[5])
    kept = (
        inputs_low,
        packed,
        short_softmax,
        long_softmax,
        context,
        first_resid,
        first_low,
        upward,
        active_low,
        second_resid,
    )
    return (outputs, kept)


def layer_backward(d_outputs, weights, kept, short_count):
    w_qkv, w_o, w_in, w_out, bias_rows, gain_rows, in_bias = weights
    (
        inputs_low,
        packed,
        short_softmax,
        long_softmax,
        context,
        first_resid,
        first_low,
        upward,
        active_low,
        second_resid,
    ) = kept
    bias_float = bias_rows.astype(jnp.float32)
    gain_float = gain_rows.astype(jnp.float32)
    row_count = d_outputs.shape[0]
    unused_second, pull_second = jax.vjp(norm_rows, second_resid, gain_float[1], bias_float[5])
    d_second, d_gain_two, d_shift_two = pull_second(d_outputs)
    d_down_low = d_second.astype(jnp.bfloat16)
    grad_out = jnp.dot(active_low.T, d_down_low, preferred_element_type=jnp.float32)
    d_active = jnp.dot(d_down_low, w_out.T, preferred_element_type=jnp.float32)
    unused_gelu, pull_gelu = jax.vjp(gelu_exact, upward)
    d_upward = pull_gelu(d_active)[0]
    d_up_low = d_upward.astype(jnp.bfloat16)
    grad_in = jnp.dot(first_low.T, d_up_low, preferred_element_type=jnp.float32)
    d_first_norm = d_second + jnp.dot(d_up_low, w_in.T, preferred_element_type=jnp.float32)
    unused_first, pull_first = jax.vjp(norm_rows, first_resid, gain_float[0], bias_float[3])
    d_first, d_gain_one, d_shift_one = pull_first(d_first_norm)
    d_att_low = d_first.astype(jnp.bfloat16)
    grad_o = jnp.dot(context.T, d_att_low, preferred_element_type=jnp.float32)
    d_context = jnp.dot(d_att_low, w_o.T, preferred_element_type=jnp.float32).astype(jnp.bfloat16)
    d_context = d_context.reshape(row_count, H, HD)
    short_pack, long_pack = split_kinds(packed, short_count)
    short_dctx, long_dctx = split_kinds(d_context, short_count)
    short_dpack = attend_back(short_pack, short_softmax, short_dctx)
    long_dpack = attend_back(long_pack, long_softmax, long_dctx)
    d_packed_low = join_kinds(short_dpack, long_dpack).reshape(row_count, -1).astype(jnp.bfloat16)
    grad_qkv = jnp.dot(inputs_low.T, d_packed_low, preferred_element_type=jnp.float32)
    d_inputs = d_first + jnp.dot(d_packed_low, w_qkv.T, preferred_element_type=jnp.float32)
    width = d_first.shape[1]
    column_sums = jnp.sum(d_packed_low.astype(jnp.float32), axis=0)
    bias_grads = jnp.stack(
        [
            column_sums[:width],
            column_sums[2 * width :],
            jnp.sum(d_first, axis=0),
            d_shift_one,
            jnp.sum(d_second, axis=0),
            d_shift_two,
        ]
    )
    gain_grads = jnp.stack([d_gain_one, d_gain_two])
    in_bias_grad = jnp.sum(d_upward, axis=0)
    return (d_inputs, (grad_qkv, grad_o, grad_in, grad_out, bias_grads, gain_grads, in_bias_grad))


def stack_member(grads_each, member):
    return jnp.stack([layer_grads[member] for layer_grads in grads_each])


def shards(
    hidden, qry_len, psg_len, qry_grad, psg_grad, w_qkv, w_o, w_in, w_out, biases, gains, in_bias
):
    layer_count = w_qkv.shape[0]
    short_count = qry_len.shape[0]
    inputs = hidden.astype(jnp.float32)
    layer_inputs = []
    fetched = []
    for which_layer in range(layer_count):
        weights = fetch_layer(w_qkv, w_o, w_in, w_out, biases, gains, in_bias, which_layer)
        layer_inputs.append(inputs)
        fetched.append(weights)
        inputs, unused_kept = layer_forward(inputs, weights, qry_len, psg_len)
    short_live = (jnp.arange(SHORT)[None, :] < qry_len[:, None]).astype(
        jnp.float32
    ) / qry_len.astype(jnp.float32)[:, None]
    long_live = (jnp.arange(LONG)[None, :] < psg_len[:, None]).astype(jnp.float32) / psg_len.astype(
        jnp.float32
    )[:, None]
    d_inputs = join_kinds(
        short_live[:, :, None] * qry_grad[:, None, :], long_live[:, :, None] * psg_grad[:, None, :]
    )
    grads_each = [None] * layer_count
    for which_layer in range(layer_count - 1, -1, -1):
        weights = fetch_layer(w_qkv, w_o, w_in, w_out, biases, gains, in_bias, which_layer)
        unused_outputs, kept = layer_forward(layer_inputs[which_layer], weights, qry_len, psg_len)
        d_inputs, local_grads = layer_backward(d_inputs, weights, kept, short_count)
        shares = (
            lax.psum_scatter(local_grads[0], "fsdp", scatter_dimension=0, tiled=True),
            lax.psum_scatter(local_grads[1], "fsdp", scatter_dimension=0, tiled=True),
            lax.psum_scatter(local_grads[2], "fsdp", scatter_dimension=0, tiled=True),
            lax.psum_scatter(local_grads[3], "fsdp", scatter_dimension=0, tiled=True),
            lax.psum_scatter(local_grads[4], "fsdp", scatter_dimension=1, tiled=True),
            lax.psum_scatter(local_grads[5], "fsdp", scatter_dimension=1, tiled=True),
            lax.psum_scatter(local_grads[6], "fsdp", scatter_dimension=0, tiled=True),
        )
        parted = (
            lax.psum_scatter(
                shares[0].astype(jnp.bfloat16), "rep", scatter_dimension=1, tiled=True
            ).astype(jnp.float32),
            lax.psum_scatter(
                shares[1].astype(jnp.bfloat16), "rep", scatter_dimension=1, tiled=True
            ).astype(jnp.float32),
            lax.psum_scatter(
                shares[2].astype(jnp.bfloat16), "rep", scatter_dimension=1, tiled=True
            ).astype(jnp.float32),
            lax.psum_scatter(
                shares[3].astype(jnp.bfloat16), "rep", scatter_dimension=1, tiled=True
            ).astype(jnp.float32),
            lax.psum_scatter(
                shares[4].astype(jnp.bfloat16), "rep", scatter_dimension=0, tiled=True
            ).astype(jnp.float32),
            lax.psum_scatter(
                shares[5].astype(jnp.bfloat16), "rep", scatter_dimension=0, tiled=True
            ).astype(jnp.float32),
            lax.psum_scatter(
                shares[6].reshape(2, -1).astype(jnp.bfloat16),
                "rep",
                scatter_dimension=0,
                tiled=True,
            ).astype(jnp.float32),
        )
        joined = (
            lax.all_gather(parted[0].astype(jnp.bfloat16), "rep", axis=1, tiled=True).astype(
                jnp.float32
            ),
            lax.all_gather(parted[1].astype(jnp.bfloat16), "rep", axis=1, tiled=True).astype(
                jnp.float32
            ),
            lax.all_gather(parted[2].astype(jnp.bfloat16), "rep", axis=1, tiled=True).astype(
                jnp.float32
            ),
            lax.all_gather(parted[3].astype(jnp.bfloat16), "rep", axis=1, tiled=True).astype(
                jnp.float32
            ),
            lax.all_gather(parted[4].astype(jnp.bfloat16), "rep", axis=0, tiled=True).astype(
                jnp.float32
            ),
            lax.all_gather(parted[5].astype(jnp.bfloat16), "rep", axis=0, tiled=True).astype(
                jnp.float32
            ),
            lax.all_gather(parted[6].astype(jnp.bfloat16), "rep", axis=0, tiled=True).astype(
                jnp.float32
            ),
        )
        grads_each[which_layer] = (
            joined[0],
            joined[1],
            joined[2],
            joined[3],
            joined[4],
            joined[5],
            joined[6].reshape(-1),
        )
    totals = tuple((stack_member(grads_each, member) for member in range(7)))
    return (
        inputs.astype(jnp.bfloat16),
        d_inputs.astype(jnp.bfloat16),
        totals[0],
        totals[1],
        totals[2],
        totals[3],
        totals[4],
        totals[5],
        totals[6],
    )


def solution(mesh):
    placed = (
        P(("rep", "fsdp"), None),
        P(("rep", "fsdp")),
        P(("rep", "fsdp")),
        P(("rep", "fsdp"), None),
        P(("rep", "fsdp"), None),
        P(None, "fsdp", None),
        P(None, "fsdp", None),
        P(None, "fsdp", None),
        P(None, "fsdp", None),
        P(None, None, "fsdp"),
        P(None, None, "fsdp"),
        P(None, "fsdp"),
    )
    return jax.shard_map(
        shards,
        mesh=mesh,
        in_specs=placed,
        out_specs=(
            P(("rep", "fsdp"), None),
            P(("rep", "fsdp"), None),
            P(None, "fsdp", None),
            P(None, "fsdp", None),
            P(None, "fsdp", None),
            P(None, "fsdp", None),
            P(None, None, "fsdp"),
            P(None, None, "fsdp"),
            P(None, "fsdp"),
        ),
        check_vma=False,
    )
```

profile of v0, /device:TPU:0, one launch (start us, length us, event | category | flops | bytes accessed | tf_op | source)
XLA Modules:
  0.0 2568.8 jit_solution(7464244133612209844)
XLA Ops:
  19.0 42.5 %all-gather.13 = bf16[16,1,192]{2,1,0:T(2,128)(2,1)S(1)} all-gather(bf16[1,1,192]{2,1,0:T(2,128)(2,1)S(1)} %get-tuple-element.119), channel_id=1, replica_groups=mesh['rep'=2,'fsdp'=16] {'fsdp'}, dimensions={0}, use_global_device_ids=true | all-gather | bytes 6528 | tf_op jit(solution)/shard_map/all_gather | solution.py:49
  62.1 35.8 %all-gather.12 = bf16[16,1,192]{2,1,0:T(2,128)(2,1)S(1)} all-gather(bf16[1,1,192]{2,1,0:T(2,128)(2,1)S(1)} %get-tuple-element.120), channel_id=1, replica_groups=mesh['rep'=2,'fsdp'=16] {'fsdp'}, dimensions={0}, use_global_device_ids=true | all-gather | bytes 6528 | tf_op jit(solution)/shard_map/all_gather | solution.py:49
  99.1 40.7 %all-gather.3 = bf16[1,2,768]{1,0,2:T(2,128)(2,1)S(1)} all-gather(bf16[1,2,48]{1,0,2:T(2,128)(2,1)S(1)} %copy.273), channel_id=5, replica_groups=mesh['rep'=2,'fsdp'=16] {'fsdp'}, dimensions={2}, use_global_device_ids=true | all-gather | bytes 3264 | tf_op jit(solution)/shard_map/all_gather | solution.py:48
  140.2 4.6 slice_reduce_fusion.9
  144.8 39.3 %all-gather.1 = bf16[1,6,768]{1,0,2:T(2,128)(2,1)S(1)} all-gather(bf16[1,6,48]{1,0,2:T(2,128)(2,1)S(1)} %copy.268), channel_id=3, replica_groups=mesh['rep'=2,'fsdp'=16] {'fsdp'}, dimensions={2}, use_global_device_ids=true | all-gather | bytes 9792 | tf_op jit(solution)/shard_map/all_gather | solution.py:47
  184.5 13.4 slice_reduce_fusion.8
  197.9 52.3 %all-gather.9 = bf16[1,2,768]{1,0,2:T(2,128)(2,1)S(1)} all-gather(bf16[1,2,48]{1,0,2:T(2,128)(2,1)S(1)} %copy.272), channel_id=11, replica_groups=mesh['rep'=2,'fsdp'=16] {'fsdp'}, dimensions={2}, use_global_device_ids=true | all-gather | bytes 3264 | tf_op jit(solution)/shard_map/all_gather | solution.py:48
  250.6 5.1 slice_reduce_fusion.1
  255.8 39.9 %all-gather.7 = bf16[1,6,768]{1,0,2:T(2,128)(2,1)S(1)} all-gather(bf16[1,6,48]{1,0,2:T(2,128)(2,1)S(1)} %copy.274), channel_id=9, replica_groups=mesh['rep'=2,'fsdp'=16] {'fsdp'}, dimensions={2}, use_global_device_ids=true | all-gather | bytes 9792 | tf_op jit(solution)/shard_map/all_gather | solution.py:47
  296.1 13.3 slice_reduce_fusion
  315.6 5.1 add_convert_fusion.1
  331.1 8.5 fusion.202
  339.5 6.8 fusion.87
  350.1 28.9 %multiply_convert_fusion.3 = (bf16[768,3072]{1,0:T(8,128)(2,1)}, f32[768,3072]{1,0:T(8,128)}, f32[768,3072]{1,0:T(8,128)}) fusion(f32[3072]{0:T(1024)S(1)} %copy-done.87, bf16[1,768,3072]{2,1,0:T(8,128)(2,1)} %all-gather.33.cloned.1.call-done, f32[768,768]{0,1:T(8,128)S(1)} %get-tuple-element.128, f32[768]{0:T(1024)S(1)} %get-tuple-element.68, ...), kind=kOutput, calls=%fused_computation.33 | convolution fusion | flops 3782541312 | bytes 30695424 | tf_op jit(solution)/shard_map/dot_general | solution.py:131
  379.0 7.8 fusion.205
  389.2 5.9 add_convert_fusion
  405.9 8.6 fusion.206
  414.5 6.7 fusion.93
  421.2 25.2 all-gather.39.cloned.1.call-done
  446.5 3.8 fusion.208
  450.6 78.6 %all-gather.41.cloned.1.call-done = bf16[1,768,3072]{2,1,0:T(8,128)(2,1)} async-done(((bf16[1,48,3072]{2,1,0:T(8,128)(2,1)}), bf16[1,768,3072]{2,1,0:T(8,128)(2,1)}) %all-gather.41.cloned.1.call-update) | async-done | bytes 4718608 | tf_op jit(solution)/shard_map/all_gather | solution.py:45
  529.2 29.3 %multiply_convert_fusion.2 = (bf16[768,3072]{1,0:T(8,128)(2,1)}, f32[768,3072]{1,0:T(8,128)}, f32[768,3072]{1,0:T(8,128)}) fusion(f32[3072]{0:T(1024)} %reshape.584, bf16[1,768,3072]{2,1,0:T(8,128)(2,1)} %all-gather.41.cloned.1.call-done, f32[768,768]{0,1:T(8,128)S(1)} %get-tuple-element.137, f32[768]{0:T(1024)} %get-tuple-element.60, ...), kind=kOutput, calls=%fused_computation.20 | convolution fusion | flops 3782541312 | bytes 30695424 | tf_op jit(solution)/shard_map/dot_general | solution.py:131
  558.5 52.6 %all-gather.43.cloned.1.call-done = bf16[1,3072,768]{2,1,0:T(8,128)(2,1)} async-done(((bf16[1,192,768]{2,1,0:T(8,128)(2,1)}), bf16[1,3072,768]{2,1,0:T(8,128)(2,1)}) %all-gather.43.cloned.1.call-update) | async-done | bytes 4718608 | tf_op jit(solution)/shard_map/all_gather | solution.py:46
  611.1 7.6 fusion.209
  624.1 15.0 fusion.210
  639.2 7.4 multiply_reduce_fusion.3
  657.3 7.9 fusion.103
  665.2 8.9 multiply_reduce_fusion.1
  674.2 6.9 multiply_convert_fusion.1
  681.1 2.9 fusion.110
  694.9 4.2 multiply_reduce_fusion.4
  699.9 15.8 fusion.211
  715.7 7.5 multiply_reduce_fusion.5
  727.9 8.4 fusion.129
  755.5 10.9 multiply_reduce_fusion
  768.4 6.8 multiply_convert_fusion
  778.3 3.2 fusion.106
  783.2 4.9 convolution_bitcast_fusion
  788.1 8.0 copy.246
  796.8 10.7 fusion.137
  808.2 10.7 fusion.138
  819.0 11.9 multiply_reduce_fusion.16
  848.8 10.7 fusion.61
  861.5 89.0 %reduce-scatter.45.cloned.1.call-done = f32[48,768]{1,0:T(8,128)} async-done(((f32[768,768]{1,0:T(8,128)}), f32[48,768]{1,0:T(8,128)}) %reduce-scatter.45.cloned.1.call-update) | async-done | bytes 147472 | tf_op jit(solution)/shard_map/reduce_scatter | solution.py:244
  952.3 154.1 %reduce-scatter.63.cloned.1.call-done = f32[48,2304]{1,0:T(8,128)} async-done(((f32[768,2304]{1,0:T(8,128)}), f32[48,2304]{1,0:T(8,128)}) %reduce-scatter.63.cloned.1.call-update) | async-done | bytes 442384
  1108.5 8.9 fusion.58
  1117.5 144.1 %reduce-scatter.61.cloned.1.call-done = f32[48,2304]{1,0:T(8,128)} async-done(((f32[768,2304]{1,0:T(8,128)}), f32[48,2304]{1,0:T(8,128)}) %reduce-scatter.61.cloned.1.call-update) | async-done | bytes 442384
  1263.8 173.6 %reduce-scatter.59.cloned.1.call-done = f32[192,768]{1,0:T(8,128)} async-done(((f32[3072,768]{1,0:T(8,128)}), f32[192,768]{1,0:T(8,128)}) %reduce-scatter.59.cloned.1.call-update) | async-done | bytes 589840 | tf_op jit(solution)/shard_map/reduce_scatter | solution.py:246
  1442.0 172.2 %reduce-scatter.57.cloned.1.call-done = f32[192,768]{1,0:T(8,128)} async-done(((f32[3072,768]{1,0:T(8,128)}), f32[192,768]{1,0:T(8,128)}) %reduce-scatter.57.cloned.1.call-update) | async-done | bytes 589840 | tf_op jit(solution)/shard_map/reduce_scatter | solution.py:246
  1616.3 7.0 add_convert_fusion.2
  1624.8 74.8 %all-reduce.8 = (bf16[3072]{0:T(1024)(128)(2,1)S(1)}, bf16[3072]{0:T(1024)(128)(2,1)S(1)}) all-reduce(f32[3072]{0:T(1024)S(1)} %copy-done.90, f32[3072]{0:T(1024)S(1)} %copy-done.91), channel_id=40, replica_groups=mesh['rep'=2,'fsdp'=16] {'fsdp'}, use_global_device_ids=true, to_apply=%region_71.72.clone | all-reduce | flops 6144 | bytes 36864
  1701.3 37.8 %reduce-scatter.79.cloned.1.call-done = f32[48,2]{1,0:T(8,128)} async-done(((f32[768,2]{1,0:T(8,128)}), f32[48,2]{1,0:T(8,128)}) %reduce-scatter.79.cloned.1.call-update) | async-done | bytes 400
  1740.0 125.2 %reduce-scatter.77.cloned.1.call-done = f32[48,2]{1,0:T(8,128)} async-done(((f32[768,2]{1,0:T(8,128)}), f32[48,2]{1,0:T(8,128)}) %reduce-scatter.77.cloned.1.call-update) | async-done | bytes 400
  1866.0 124.3 %reduce-scatter.75.cloned.1.call-done = f32[48,6]{1,0:T(8,128)} async-done(((f32[768,6]{1,0:T(8,128)}), f32[48,6]{1,0:T(8,128)}) %reduce-scatter.75.cloned.1.call-update) | async-done | bytes 1168
  1991.1 125.2 %reduce-scatter.73.cloned.1.call-done = f32[48,6]{1,0:T(8,128)} async-done(((f32[768,6]{1,0:T(8,128)}), f32[48,6]{1,0:T(8,128)}) %reduce-scatter.73.cloned.1.call-update) | async-done | bytes 1168
  2121.6 170.6 %reduce-scatter.53.cloned.1.call-done = f32[48,3072]{1,0:T(8,128)} async-done(((f32[768,3072]{1,0:T(8,128)}), f32[48,3072]{1,0:T(8,128)}) %reduce-scatter.53.cloned.1.call-update) | async-done | bytes 589840 | tf_op jit(solution)/shard_map/reduce_scatter | solution.py:245
  2308.3 4.2 reduce-scatter.65.cloned.1.call-done
  2317.9 6.7 reduce-scatter.43.cloned.1.call-done
  2327.1 175.5 %reduce-scatter.49.cloned.1.call-done = f32[48,3072]{1,0:T(8,128)} async-done(((f32[768,3072]{1,0:T(8,128)}), f32[48,3072]{1,0:T(8,128)}) %reduce-scatter.49.cloned.1.call-update) | async-done | bytes 589840 | tf_op jit(solution)/shard_map/reduce_scatter | solution.py:245
  2504.4 7.3 reduce-scatter.41.cloned.1.call-done
  2515.6 7.4 reduce-scatter.71.cloned.1.call-done
  2524.0 10.1 reduce-scatter.69.cloned.1.call-done
  2539.2 6.4 reduce-scatter.55.cloned.1.call-done
  2547.9 9.4 reduce-scatter.51.cloned.1.call-done
  (544 shorter events, 191.4 us)
Async XLA Ops:
  7.2 308.4 %all-gather.29.cloned.1.call-start = ((), (), s32[]{:S(2)}) async-start(), calls=%async_computation.30 | async-start | bytes 3760128 | tf_op jit(solution)/shard_map/all_gather | solution.py:43
  9.2 337.2 %all-gather.31.cloned.1.call-start = ((), (), s32[]{:S(2)}) async-start(), calls=%async_computation.31 | async-start | bytes 1253376 | tf_op jit(solution)/shard_map/all_gather | solution.py:44
  10.8 339.3 %all-gather.33.cloned.1.call-start = ((), (), s32[]{:S(2)}) async-start(), calls=%async_computation.32 | async-start | bytes 5013504 | tf_op jit(solution)/shard_map/all_gather | solution.py:45
  12.8 366.2 %all-gather.35.cloned.1.call-start = ((), (), s32[]{:S(2)}) async-start(), calls=%async_computation.33 | async-start | bytes 5013504 | tf_op jit(solution)/shard_map/all_gather | solution.py:46
  13.7 375.5 %all-gather.37.cloned.1.call-start = ((), (), s32[]{:S(2)}) async-start(), calls=%async_computation.34 | async-start | bytes 3760128 | tf_op jit(solution)/shard_map/all_gather | solution.py:43
  14.3 432.2 %all-gather.39.cloned.1.call-start = ((), (), s32[]{:S(2)}) async-start(), calls=%async_computation.35 | async-start | bytes 1253376 | tf_op jit(solution)/shard_map/all_gather | solution.py:44
  14.9 514.3 %all-gather.41.cloned.1.call-start = ((), (), s32[]{:S(2)}) async-start(), calls=%async_computation.36 | async-start | bytes 5013504 | tf_op jit(solution)/shard_map/all_gather | solution.py:45
  15.6 595.5 %all-gather.43.cloned.1.call-start = ((), (), s32[]{:S(2)}) async-start(), calls=%async_computation.37 | async-start | bytes 5013504 | tf_op jit(solution)/shard_map/all_gather | solution.py:46
  16.4 843.3 %reduce-scatter.47.cloned.1.call-start = ((), (), s32[]{:S(2)}) async-start(), calls=%async_computation.23 | async-start | bytes 2506752 | tf_op jit(solution)/shard_map/reduce_scatter | solution.py:244
  144.8 234.2 %copy-start.59 = (f32[768]{0:T(1024)}, f32[768]{0:T(1024)S(1)}, u32[]{:S(2)}) copy-start(f32[768]{0:T(1024)S(1)} %get-tuple-element.65) | copy-start | bytes 9220
  144.8 301.7 %copy-start.63 = (f32[768]{0:T(1024)}, f32[768]{0:T(1024)S(1)}, u32[]{:S(2)}) copy-start(f32[768]{0:T(1024)S(1)} %get-tuple-element.64) | copy-start | bytes 9220
  197.9 181.1 %copy-start.98 = (f32[768]{0:T(1024)}, f32[768]{0:T(1024)S(1)}, u32[]{:S(2)}) copy-start(f32[768]{0:T(1024)S(1)} %get-tuple-element.68) | copy-start | bytes 9220
  197.9 248.5 %copy-start.101 = (f32[768]{0:T(1024)}, f32[768]{0:T(1024)S(1)}, u32[]{:S(2)}) copy-start(f32[768]{0:T(1024)S(1)} %get-tuple-element.66) | copy-start | bytes 9220
  250.6 58.8 %copy-start.97 = (f32[2,768]{1,0:T(2,128)S(1)}, f32[2,768]{1,0:T(2,128)}, u32[]{:S(2)}) copy-start(f32[2,768]{1,0:T(2,128)} %param.15) | copy-start | bytes 18436
  250.6 59.0 %copy-start.32 = (bf16[768,768]{1,0:T(8,128)(2,1)S(1)}, bf16[768,768]{1,0:T(8,128)(2,1)}, u32[]{:S(2)}) copy-start(bf16[768,768]{1,0:T(8,128)(2,1)} %param.12) | copy-start | bytes 3538948
  349.2 29.8 %copy-start.1 = (f32[768,768]{0,1:T(8,128)}, f32[768,768]{0,1:T(8,128)S(1)}, u32[]{:S(2)}) copy-start(f32[768,768]{0,1:T(8,128)S(1)} %get-tuple-element.128) | copy-start | bytes 7077892
  349.2 29.8 %copy-start.43 = (f32[768]{0:T(1024)}, f32[768]{0:T(1024)S(1)}, u32[]{:S(2)}) copy-start(f32[768]{0:T(1024)S(1)} %broadcast_multiply_fusion.4) | copy-start | bytes 9220
  350.1 28.9 %copy-start.67 = (f32[768]{0:T(1024)}, f32[768]{0:T(1024)S(1)}, u32[]{:S(2)}) copy-start(f32[768]{0:T(1024)S(1)} %fusion.151) | copy-start | bytes 9220
  350.1 28.9 %copy-start.102 = (f32[768]{0:T(1024)S(1)}, f32[768]{0:T(1024)}, u32[]{:S(2)}) copy-start(f32[768]{0:T(1024)} %get-tuple-element.67) | copy-start | bytes 9220
  386.9 59.6 %copy-start.47 = (f32[768]{0:T(1024)}, f32[768]{0:T(1024)S(1)}, u32[]{:S(2)}) copy-start(f32[768]{0:T(1024)S(1)} %broadcast_multiply_fusion.3) | copy-start | bytes 9220
  389.2 57.3 %copy-start.82 = (f32[768]{0:T(1024)}, f32[768]{0:T(1024)S(1)}, u32[]{:S(2)}) copy-start(f32[768]{0:T(1024)S(1)} %fusion.152) | copy-start | bytes 9220
  450.3 196.3 %copy-start.3 = (f32[768,768]{0,1:T(8,128)}, f32[768,768]{0,1:T(8,128)S(1)}, u32[]{:S(2)}) copy-start(f32[768,768]{0,1:T(8,128)S(1)} %get-tuple-element.137) | copy-start | bytes 7077892
  450.3 78.9 %copy-start.61 = (f32[768]{0:T(1024)S(1)}, f32[768]{0:T(1024)}, u32[]{:S(2)}) copy-start(f32[768]{0:T(1024)} %get-tuple-element.57) | copy-start | bytes 9220
  450.3 196.3 %copy-start.45 = (f32[768]{0:T(1024)}, f32[768]{0:T(1024)S(1)}, u32[]{:S(2)}) copy-start(f32[768]{0:T(1024)S(1)} %broadcast_multiply_fusion.2) | copy-start | bytes 9220
  450.6 196.0 %copy-start.70 = (f32[768]{0:T(1024)}, f32[768]{0:T(1024)S(1)}, u32[]{:S(2)}) copy-start(f32[768]{0:T(1024)S(1)} %fusion.153) | copy-start | bytes 9220
  621.9 17.3 slice-start.8
  657.3 16.9 slice-start.3
  657.3 16.9 slice-start.4
  690.3 260.2 %reduce-scatter.45.cloned.1.call-start = ((), (), s32[]{:S(2)}) async-start(), calls=%async_computation.22 | async-start | bytes 2506752 | tf_op jit(solution)/shard_map/reduce_scatter | solution.py:244
  691.9 36.0 %copy-start.24 = (bf16[256,3,12,64]{0,3,2,1:T(8,128)(2,1)}, bf16[256,3,12,64]{0,3,2,1:T(8,128)(2,1)S(1)}, u32[]{:S(2)}) copy-start(bf16[256,3,12,64]{0,3,2,1:T(8,128)(2,1)S(1)} %pad_maximum_fusion.7) | copy-start | bytes 3538948
  699.2 16.5 slice-start.6
  699.8 15.9 copy-start.13
  699.8 15.8 copy-start.84
  699.9 15.8 copy-start.2
  699.9 15.8 copy-start.44
  699.9 15.8 copy-start.60
  699.9 15.8 copy-start.68
  699.9 15.8 slice-start.7
  727.8 378.5 %reduce-scatter.63.cloned.1.call-start = ((), (), s32[]{:S(2)}) async-start(), calls=%async_computation.39 | async-start | bytes 7520256
  736.3 525.3 %reduce-scatter.61.cloned.1.call-start = ((), (), s32[]{:S(2)}) async-start(), calls=%async_computation.38 | async-start | bytes 7520256
  755.0 84.2 %copy-start.23 = (bf16[256,3,12,64]{0,3,2,1:T(8,128)(2,1)}, bf16[256,3,12,64]{0,3,2,1:T(8,128)(2,1)S(1)}, u32[]{:S(2)}) copy-start(bf16[256,3,12,64]{0,3,2,1:T(8,128)(2,1)S(1)} %pad_maximum_fusion.8) | copy-start | bytes 3538948
  796.2 641.2 %reduce-scatter.59.cloned.1.call-start = ((), (), s32[]{:S(2)}) async-start(), calls=%async_computation.29 | async-start | bytes 10027008 | tf_op jit(solution)/shard_map/reduce_scatter | solution.py:246
  807.6 806.6 %reduce-scatter.57.cloned.1.call-start = ((), (), s32[]{:S(2)}) async-start(), calls=%async_computation.28 | async-start | bytes 10027008 | tf_op jit(solution)/shard_map/reduce_scatter | solution.py:246
  818.9 920.2 %reduce-scatter.79.cloned.1.call-start = ((), (), s32[]{:S(2)}) async-start(), calls=%async_computation.47 | async-start | bytes 417792
  841.3 1023.9 %reduce-scatter.77.cloned.1.call-start = ((), (), s32[]{:S(2)}) async-start(), calls=%async_computation.46 | async-start | bytes 417792
  842.3 1148.0 %reduce-scatter.75.cloned.1.call-start = ((), (), s32[]{:S(2)}) async-start(), calls=%async_computation.45 | async-start | bytes 417792
  845.5 1270.8 %reduce-scatter.73.cloned.1.call-start = ((), (), s32[]{:S(2)}) async-start(), calls=%async_computation.44 | async-start | bytes 417792
  848.6 1443.6 %reduce-scatter.53.cloned.1.call-start = ((), (), s32[]{:S(2)}) async-start(), calls=%async_computation.26 | async-start | bytes 10027008 | tf_op jit(solution)/shard_map/reduce_scatter | solution.py:245
  859.6 248.9 %copy-start.69 = (f32[768]{0:T(1024)S(1)}, f32[768]{0:T(1024)}, u32[]{:S(2)}) copy-start(f32[768]{0:T(1024)} %copy-done.67) | copy-start | bytes 9220
  859.6 248.9 %copy-start.99 = (f32[768]{0:T(1024)S(1)}, f32[768]{0:T(1024)}, u32[]{:S(2)}) copy-start(f32[768]{0:T(1024)} %copy-done.98) | copy-start | bytes 9220
  859.6 1447.7 %reduce-scatter.67.cloned.1.call-start = ((), (), s32[]{:S(2)}) async-start(), calls=%async_computation.41 | async-start | bytes 294912
  861.5 1451.1 %reduce-scatter.65.cloned.1.call-start = ((), (), s32[]{:S(2)}) async-start(), calls=%async_computation.40 | async-start | bytes 294912
  952.2 1372.4 %reduce-scatter.43.cloned.1.call-start = ((), (), s32[]{:S(2)}) async-start(), calls=%async_computation.21 | async-start | bytes 884736 | tf_op jit(solution)/shard_map/reduce_scatter | solution.py:252
  1108.4 1394.1 %reduce-scatter.49.cloned.1.call-start = ((), (), s32[]{:S(2)}) async-start(), calls=%async_computation.24 | async-start | bytes 10027008 | tf_op jit(solution)/shard_map/reduce_scatter | solution.py:245
  1117.4 322.0 %copy-start.116 = (u32[32]{0:T(128)S(1)}, u32[32]{0:T(128)}, u32[]{:S(2)}) copy-start(u32[32]{0:T(128)} %constant.121) | copy-start | bytes 388
  1117.4 322.6 %copy-start.115 = (u32[32]{0:T(128)S(1)}, u32[32]{0:T(128)}, u32[]{:S(2)}) copy-start(u32[32]{0:T(128)} %constant.105) | copy-start | bytes 388
  1117.5 1394.3 %reduce-scatter.41.cloned.1.call-start = ((), (), s32[]{:S(2)}) async-start(), calls=%async_computation.20 | async-start | bytes 884736 | tf_op jit(solution)/shard_map/reduce_scatter | solution.py:252
  1263.7 352.6 %copy-start.5 = (f32[768,768]{0,1:T(8,128)S(1)}, f32[768,768]{0,1:T(8,128)}, u32[]{:S(2)}) copy-start(f32[768,768]{0,1:T(8,128)} %copy-done.4) | copy-start | bytes 7077892
  1263.7 352.6 %copy-start.75 = (f32[768]{0:T(1024)S(1)}, f32[768]{0:T(1024)}, u32[]{:S(2)}) copy-start(f32[768]{0:T(1024)} %copy-done.72) | copy-start | bytes 9220
  1263.7 1259.2 %reduce-scatter.71.cloned.1.call-start = ((), (), s32[]{:S(2)}) async-start(), calls=%async_computation.43 | async-start | bytes 589824
  1439.4 1094.7 %reduce-scatter.69.cloned.1.call-start = ((), (), s32[]{:S(2)}) async-start(), calls=%async_computation.42 | async-start | bytes 589824
  1616.2 929.4 %reduce-scatter.55.cloned.1.call-start = ((), (), s32[]{:S(2)}) async-start(), calls=%async_computation.27 | async-start | bytes 442368 | tf_op jit(solution)/shard_map/reduce_scatter | solution.py:258
  1623.3 76.6 %copy-start.35 = (bf16[768,768]{0,1:T(8,128)(2,1)S(1)}, bf16[768,768]{0,1:T(8,128)(2,1)}, u32[]{:S(2)}) copy-start(bf16[768,768]{0,1:T(8,128)(2,1)} %add_convert_fusion.2) | copy-start | bytes 3538948
  2294.0 263.3 %reduce-scatter.51.cloned.1.call-start = ((), (), s32[]{:S(2)}) async-start(), calls=%async_computation.25 | async-start | bytes 442368 | tf_op jit(solution)/shard_map/reduce_scatter | solution.py:258
  (94 other events, 379.6 us)
Sparse Core Ops, SparseCore 0:
  11.4 74.3 all-gather.28
  88.6 55.9 all-gather.30
  148.0 85.0 all-gather.32
  236.3 79.8 all-gather.34
  318.8 70.2 all-gather.36
  391.8 54.6 all-gather.38
  449.8 79.3 all-gather.40
  532.0 79.0 all-gather.42
  690.5 126.8 reduce-scatter.46
  822.9 127.5 reduce-scatter.44
  955.8 150.4 reduce-scatter.62
  1111.5 149.9 reduce-scatter.60
  1267.3 170.0 reduce-scatter.58
  1443.8 170.2 reduce-scatter.56
  1618.6 120.4 reduce-scatter.78
  1744.4 120.7 reduce-scatter.76
  1869.6 120.6 reduce-scatter.74
  1995.5 120.7 reduce-scatter.72
  2122.0 170.1 reduce-scatter.52
  2294.9 6.4 reduce-scatter.66
  2303.8 8.7 reduce-scatter.64
  2315.5 9.1 reduce-scatter.42
  2330.3 172.1 reduce-scatter.48
  2504.8 6.9 reduce-scatter.40
  2514.0 8.9 reduce-scatter.70
  2525.1 8.9 reduce-scatter.68
  2536.8 8.8 reduce-scatter.54
  2548.4 8.8 reduce-scatter.50
where the time goes:
time: 2580 us; the launch traced here: 2570 us
  waiting for transfers between devices  1700 us (66%)
  blocking collectives  355 us (14%)
  matrix products  297 us (12%)
  local copies, waits for them, and re-layouts  127 us (5%)
  other arithmetic  65.9 us (3%)
    unnamed x38, waiting for transfers between devices  735 us
    reduce_scatter x2, waiting for transfers between devices, shards(): lax.psum_scatter(local_grads[2], 'fsdp', scatter_dimension=0, tiled=True)  346 us
    reduce_scatter x2, waiting for transfers between devices, shards(): lax.psum_scatter(local_grads[3], 'fsdp', scatter_dimension=0, tiled=True)  346 us
    all_gather x2, blocking collectives, fetch_layer(): lax.all_gather(gains[which_layer], 'fsdp', axis=1, tiled=True)  92.9 us
    reduce_scatter x2, waiting for transfers between devices, shards(): lax.psum_scatter(local_grads[1], 'fsdp', scatter_dimension=0, tiled=True)  89 us
    all_gather x2, blocking collectives, fetch_layer(): lax.all_gather(biases[which_layer], 'fsdp', axis=1, tiled=True)  79.3 us
    all_gather x2, waiting for transfers between devices, fetch_layer(): lax.all_gather(w_in[which_layer], 'fsdp', axis=0, tiled=True)  78.6 us
    all_gather x2, blocking collectives, fetch_layer(): lax.all_gather(bias_rows, 'fsdp', axis=0, tiled=True)  78.3 us
  transfers between devices with their start and end apart: 28, of which 21 were waited for; matrix products, arithmetic and copies ran while one was open for 15% of the time, Pallas kernels for 0%

commit v1 on v0

--- a/solution.py
+++ b/solution.py
@@ -1,12 +1,418 @@
+import functools
 import jax
 import jax.numpy as jnp
 from jax import lax
+from jax.experimental import pallas as pl
+from jax.experimental.pallas import tpu as pltpu
+
 from jax.sharding import PartitionSpec as P
 
+MESH = pl.DeviceIdType.MESH
+D = 768
 H = 12
 HD = 64
 SHORT = 128
 LONG = 512
+BLK = 16
+PAIR = 2 * BLK
+LAG = 2
+DEPTH = 4
+ROUTES = (
+    ("xzy", 0, 128),
+    ("yzx", 128, 128),
+    ("zxy", 256, 256),
+    ("zyx", 512, 256),
+)
+
+
+def place():
+    core = lax.axis_index("rep")
+    spot = lax.axis_index("fsdp")
+    return core, lax.rem(spot, 2), lax.rem(spot // 2, 2), spot // 4
+
+
+def partner(axis, step=1):
+    core, x, y, z = place()
+    if axis == "c":
+        core = 1 - core
+    elif axis == "x":
+        x = 1 - x
+    elif axis == "y":
+        y = 1 - y
+    else:
+        z = lax.rem(z + step, 4)
+    return (core, z * 4 + y * 2 + x)
+
+
+def greet():
+    barrier = pltpu.get_barrier_semaphore()
+    others = [("c", 1), ("x", 1), ("y", 1), ("z", 1), ("z", 2), ("z", 3)]
+    for axis, step in others:
+        pl.semaphore_signal(
+            barrier, inc=1, device_id=partner(axis, step), device_id_type=MESH
+        )
+    pl.semaphore_wait(barrier, len(others))
+
+
+def steps_of(axis):
+    return (1, 2, 3) if axis == "z" else (1,)
+
+
+SLOTS = {}
+for _route, (_order, _a, _b) in enumerate(ROUTES):
+    for _stage in range(3):
+        for _step in steps_of(_order[_stage]):
+            SLOTS[(_route, _stage, _step)] = len(SLOTS)
+CORE_SLOT = len(SLOTS)
+FINAL_SLOT = CORE_SLOT + 1
+SLOT_COUNT = CORE_SLOT + 2
+
+
+def when_in(chunk, count, work):
+    if isinstance(chunk, int):
+        if 0 <= chunk < count:
+            work()
+    else:
+        pl.when(jnp.logical_and(chunk >= 0, chunk < count))(work)
+
+
+def gather_rows(chunk, core, count):
+    spot = lax.rem(chunk + count - 1, count)
+    return pl.ds(pl.multiple_of(spot * PAIR + core * BLK, BLK), BLK)
+
+
+def scatter_rows(chunk, core, count):
+    spot = lax.rem(2 * count - 2 - chunk, count)
+    return pl.ds(pl.multiple_of(spot * PAIR + core * BLK, BLK), BLK)
+
+
+class Gather:
+    def __init__(self, own, whole, send, recv, local, count):
+        self.own, self.whole, self.send, self.recv = own, whole, send, recv
+        self.local = local
+        self.count = count
+        self.rounds = count + 4 * LAG
+
+    def copies(self, chunk, stage):
+        core, x, y, z = place()
+        slot = lax.rem(chunk, DEPTH)
+        if stage == 3:
+            rows = gather_rows(chunk, core, self.count)
+            part = self.whole.at[:, :, :, rows, :]
+            return [
+                pltpu.make_async_remote_copy(
+                    src_ref=part,
+                    dst_ref=part,
+                    send_sem=self.send.at[CORE_SLOT, slot],
+                    recv_sem=self.recv.at[CORE_SLOT, slot],
+                    device_id=partner("c"),
+                    device_id_type=MESH,
+                )
+            ]
+        rows = gather_rows(chunk, core, self.count)
+        found = []
+        for route, (order, first, width) in enumerate(ROUTES):
+            axis = order[stage]
+            done = order[:stage]
+            columns = pl.ds(first, width)
+            spans = [
+                pl.ds(0, size) if name in done else pl.ds(at, 1)
+                for name, at, size in (("z", z, 4), ("y", y, 2), ("x", x, 2))
+            ]
+            part = self.whole.at[spans[0], spans[1], spans[2], rows, columns]
+            if stage == 0:
+                source = self.own.at[rows, columns]
+                part = self.whole.at[z, y, x, rows, columns]
+            else:
+                source = part
+            for step in steps_of(axis):
+                index = SLOTS[(route, stage, step)]
+                found.append(
+                    pltpu.make_async_remote_copy(
+                        src_ref=source,
+                        dst_ref=part,
+                        send_sem=self.send.at[index, slot],
+                        recv_sem=self.recv.at[index, slot],
+                        device_id=partner(axis, step),
+                        device_id_type=MESH,
+                    )
+                )
+        return found
+
+    def keep(self, chunk):
+        core, x, y, z = place()
+        rows = gather_rows(chunk, core, self.count)
+        return pltpu.make_async_copy(
+            self.own.at[rows, :],
+            self.whole.at[z, y, x, rows, :],
+            self.local.at[lax.rem(chunk, DEPTH)],
+        )
+
+    def round(self, number):
+        for stage in range(4):
+            chunk = number - LAG * stage - LAG
+
+            def finish(chunk=chunk, stage=stage):
+                for copy in self.copies(chunk, stage):
+                    copy.wait()
+                if stage == 0:
+                    self.keep(chunk).wait()
+
+            when_in(chunk, self.count, finish)
+        for stage in range(4):
+            chunk = number - LAG * stage
+
+            def begin(chunk=chunk, stage=stage):
+                for copy in self.copies(chunk, stage):
+                    copy.start()
+                if stage == 0:
+                    self.keep(chunk).start()
+
+            when_in(chunk, self.count, begin)
+
+
+def gather_kernel(count, own, whole, send, recv, local):
+    greet()
+    rounds = Gather(own, whole, send, recv, local, count)
+
+    def body(number, carry):
+        rounds.round(number)
+        return carry
+
+    lax.fori_loop(0, rounds.rounds, body, 0)
+
+
+def gather(own):
+    rows = own.shape[0]
+    return pl.pallas_call(
+        functools.partial(gather_kernel, rows // PAIR),
+        out_shape=jax.ShapeDtypeStruct((4, 2, 2, rows, D), own.dtype),
+        in_specs=[pl.BlockSpec(memory_space=pl.ANY)],
+        out_specs=pl.BlockSpec(memory_space=pl.ANY),
+        scratch_shapes=[
+            pltpu.SemaphoreType.DMA((SLOT_COUNT, DEPTH)),
+            pltpu.SemaphoreType.DMA((SLOT_COUNT, DEPTH)),
+            pltpu.SemaphoreType.DMA((DEPTH,)),
+        ],
+        compiler_params=pltpu.CompilerParams(
+            collective_id=0, has_side_effects=True, vmem_limit_bytes=48 * 2**20
+        ),
+        name="gather_weights",
+    )(own)
+
+
+class Scatter:
+    def __init__(self, partial, total, work, send, recv, local, count):
+        self.partial, self.total, self.work = partial, total, work
+        self.send, self.recv, self.local = send, recv, local
+        self.count = count
+        self.rounds = count + 5 * LAG
+
+    def rows(self, chunk, core):
+        return scatter_rows(chunk, core, self.count)
+
+    def load(self, chunk):
+        core = place()[0]
+        slot = lax.rem(chunk, DEPTH)
+        return pltpu.make_async_copy(
+            self.partial.at[:, :, :, self.rows(chunk, core), :],
+            self.work["mine"].at[slot],
+            self.local.at[0, slot],
+        )
+
+    def store(self, chunk):
+        core = place()[0]
+        slot = lax.rem(chunk, DEPTH)
+        return pltpu.make_async_copy(
+            self.work["final"].at[slot],
+            self.total.at[self.rows(chunk, core), :],
+            self.local.at[1, slot],
+        )
+
+    def remote(self, src, dst, index, slot, device):
+        return pltpu.make_async_remote_copy(
+            src_ref=src,
+            dst_ref=dst,
+            send_sem=self.send.at[index, slot],
+            recv_sem=self.recv.at[index, slot],
+            device_id=device,
+            device_id_type=MESH,
+        )
+
+    def copies(self, chunk, stage):
+        core, x, y, z = place()
+        slot = lax.rem(chunk, DEPTH)
+        if stage == 0:
+            return [
+                self.remote(
+                    self.partial.at[:, :, :, self.rows(chunk, 1 - core), :],
+                    self.work["theirs"].at[slot],
+                    CORE_SLOT,
+                    slot,
+                    partner("c"),
+                )
+            ]
+        if stage == 4:
+            return [
+                self.remote(
+                    self.work["final"].at[slot],
+                    self.total.at[self.rows(chunk, core), :],
+                    FINAL_SLOT,
+                    slot,
+                    partner("c"),
+                )
+            ]
+        found = []
+        at = {"x": x, "y": y, "z": z}
+        for route, (gather_order, first, width) in enumerate(ROUTES):
+            order = gather_order[::-1]
+            axis = order[stage - 1]
+            left = [name for name in "zyx" if name not in order[: stage - 1]]
+            if stage == 1:
+                held = self.work["pair"].at[slot]
+                columns = pl.ds(first, width)
+            else:
+                held = self.work["held", route, stage - 1].at[slot]
+                columns = slice(None)
+            landing = self.work["land", route, stage].at[slot]
+            for step in steps_of(axis):
+                if axis == "z":
+                    to = lax.rem(z + step, 4)
+                else:
+                    to = 1 - at[axis]
+                index = tuple(to if name == axis else slice(None) for name in left)
+                found.append(
+                    self.remote(
+                        held.at[index + (slice(None), columns)],
+                        landing.at[step - 1] if axis == "z" else landing,
+                        SLOTS[(route, 3 - stage, step)],
+                        slot,
+                        partner(axis, step),
+                    )
+                )
+        return found
+
+    def add(self, chunk, stage):
+        core, x, y, z = place()
+        slot = lax.rem(chunk, DEPTH)
+        wide = jnp.float32
+        if stage == 0:
+            mine, theirs, pair = (self.work[k] for k in ("mine", "theirs", "pair"))
+
+            def one(which, carry):
+                a, b, c = which // 4, lax.rem(which // 2, 2), lax.rem(which, 2)
+                pair[slot, a, b, c] = (
+                    mine[slot, a, b, c].astype(wide) + theirs[slot, a, b, c].astype(wide)
+                ).astype(pair.dtype)
+                return carry
+
+            lax.fori_loop(0, 16, one, 0)
+            return
+        at = {"x": x, "y": y, "z": z}
+        for route, (gather_order, first, width) in enumerate(ROUTES):
+            order = gather_order[::-1]
+            axis = order[stage - 1]
+            left = [name for name in "zyx" if name not in order[: stage - 1]]
+            if stage == 1:
+                held, columns = self.work["pair"], slice(first, first + width)
+            else:
+                held, columns = self.work["held", route, stage - 1], slice(None)
+            index = tuple(at[axis] if name == axis else slice(None) for name in left)
+            value = held[(slot,) + index + (slice(None), columns)].astype(wide)
+            landing = self.work["land", route, stage]
+            if axis == "z":
+                for step in (1, 2, 3):
+                    value = value + landing[slot, step - 1].astype(wide)
+            else:
+                value = value + landing[slot].astype(wide)
+            if stage == 3:
+                self.work["final"][slot, :, first : first + width] = value
+            else:
+                kept = self.work["held", route, stage]
+                kept[slot] = value.astype(kept.dtype)
+
+    def round(self, number):
+        for stage in range(5):
+            chunk = number - LAG * stage - LAG
+
+            def finish(chunk=chunk, stage=stage):
+                for copy in self.copies(chunk, stage):
+                    copy.wait()
+                if stage == 0:
+                    self.load(chunk).wait()
+                if stage == 4:
+                    self.store(chunk).wait()
+                else:
+                    self.add(chunk, stage)
+
+            when_in(chunk, self.count, finish)
+        for stage in range(5):
+            chunk = number - LAG * stage
+
+            def begin(chunk=chunk, stage=stage):
+                for copy in self.copies(chunk, stage):
+                    copy.start()
+                if stage == 0:
+                    self.load(chunk).start()
+                if stage == 4:
+                    self.store(chunk).start()
+
+            when_in(chunk, self.count, begin)
+
+
+def scatter_scratch():
+    low = jnp.bfloat16
+    shapes = {
+        "mine": ((4, 2, 2, BLK, D), low),
+        "theirs": ((4, 2, 2, BLK, D), low),
+        "pair": ((4, 2, 2, BLK, D), low),
+        "final": ((BLK, D), jnp.float32),
+    }
+    size = {"z": 4, "y": 2, "x": 2}
+    for route, (gather_order, first, width) in enumerate(ROUTES):
+        order = gather_order[::-1]
+        for stage in (1, 2, 3):
+            axis = order[stage - 1]
+            left = tuple(size[n] for n in "zyx" if n not in order[:stage])
+            steps = (3,) if axis == "z" else ()
+            shapes["land", route, stage] = (steps + left + (BLK, width), low)
+            if stage < 3:
+                shapes["held", route, stage] = (left + (BLK, width), low)
+    return shapes
+
+
+def scatter_kernel(count, names, partial, total, send, recv, local, *buffers):
+    greet()
+    rounds = Scatter(
+        partial, total, dict(zip(names, buffers)), send, recv, local, count
+    )
+
+    def body(number, carry):
+        rounds.round(number)
+        return carry
+
+    lax.fori_loop(0, rounds.rounds, body, 0)
+
+
+def scatter(partial):
+    rows = partial.shape[3]
+    shapes = scatter_scratch()
+    return pl.pallas_call(
+        functools.partial(scatter_kernel, rows // PAIR, tuple(shapes)),
+        out_shape=jax.ShapeDtypeStruct((rows, D), jnp.float32),
+        in_specs=[pl.BlockSpec(memory_space=pl.ANY)],
+        out_specs=pl.BlockSpec(memory_space=pl.ANY),
+        scratch_shapes=[
+            pltpu.SemaphoreType.DMA((SLOT_COUNT, DEPTH)),
+            pltpu.SemaphoreType.DMA((SLOT_COUNT, DEPTH)),
+            pltpu.SemaphoreType.DMA((2, DEPTH)),
+        ]
+        + [pltpu.VMEM((DEPTH,) + s, t) for s, t in shapes.values()],
+        compiler_params=pltpu.CompilerParams(
+            collective_id=1, has_side_effects=True, vmem_limit_bytes=48 * 2**20
+        ),
+        name="sum_gradients",
+    )(partial)
 
 
 NORM_EPS = 1e-12
@@ -35,28 +441,6 @@
     short_flat = short_part.reshape((-1,) + short_part.shape[2:])
     long_flat = long_part.reshape((-1,) + long_part.shape[2:])
     return jnp.concatenate([short_flat, long_flat], axis=0)
-
-
-def fetch_layer(w_qkv, w_o, w_in, w_out, biases, gains, in_bias, which_layer):
-    bias_rows = in_bias[which_layer].reshape(1, -1)
-    complete = (
-        lax.all_gather(w_qkv[which_layer], "fsdp", axis=0, tiled=True),
-        lax.all_gather(w_o[which_layer], "fsdp", axis=0, tiled=True),
-        lax.all_gather(w_in[which_layer], "fsdp", axis=0, tiled=True),
-        lax.all_gather(w_out[which_layer], "fsdp", axis=0, tiled=True),
-        lax.all_gather(biases[which_layer], "fsdp", axis=1, tiled=True),
-        lax.all_gather(gains[which_layer], "fsdp", axis=1, tiled=True),
-        lax.all_gather(bias_rows, "fsdp", axis=0, tiled=True),
-    )
-    return (
-        complete[0],
-        complete[1],
-        complete[2],
-        complete[3],
-        complete[4],
-        complete[5],
-        complete[6].reshape(-1),
-    )
 
 
 def attend_kind(packed, lengths):
@@ -208,23 +592,74 @@
     return (d_inputs, (grad_qkv, grad_o, grad_in, grad_out, bias_grads, gain_grads, in_bias_grad))
 
 
-def stack_member(grads_each, member):
-    return jnp.stack([layer_grads[member] for layer_grads in grads_each])
+def pack_own(w_qkv, w_o, w_in, w_out, biases, gains, in_bias):
+    layers, part = w_qkv.shape[0], w_qkv.shape[1]
+    pieces = []
+    for layer in range(layers):
+        for weight in (w_qkv[layer], w_o[layer], w_in[layer]):
+            panels = weight.reshape(part, -1, D).transpose(1, 0, 2)
+            pieces.append(panels.reshape(-1, D))
+        pieces.append(w_out[layer])
+    small = jnp.concatenate([biases.reshape(-1), gains.reshape(-1), in_bias.reshape(-1)])
+    block = PAIR * D
+    small = jnp.pad(small, (0, -small.shape[0] % block))
+    pieces.append(small.reshape(-1, D))
+    return jnp.concatenate(pieces, axis=0)
+
+
+def small_parts(rows, parts, layers, part, hidden_part):
+    flat = rows.reshape(parts, -1)
+    cuts = (layers * 6 * part, layers * 8 * part, layers * (8 * part + hidden_part))
+    biases = flat[:, : cuts[0]].reshape(parts, layers, 6, part)
+    gains = flat[:, cuts[0] : cuts[1]].reshape(parts, layers, 2, part)
+    in_bias = flat[:, cuts[1] : cuts[2]].reshape(parts, layers, hidden_part)
+    return (
+        biases.transpose(1, 2, 0, 3).reshape(layers, 6, -1),
+        gains.transpose(1, 2, 0, 3).reshape(layers, 2, -1),
+        in_bias.transpose(1, 0, 2).reshape(layers, -1),
+    )
+
+
+def layer_rows(part):
+    return (0, 3 * part, 4 * part, 8 * part, 12 * part)
 
 
 def shards(
-    hidden, qry_len, psg_len, qry_grad, psg_grad, w_qkv, w_o, w_in, w_out, biases, gains, in_bias
+    hidden, qry_len, psg_len, qry_grad, psg_grad, w_qkv, w_o, w_in, w_out, biases, gains, in_bias, parts, near
 ):
-    layer_count = w_qkv.shape[0]
+    layers, part, hidden_part = w_qkv.shape[0], w_qkv.shape[1], w_out.shape[1]
+    cuts = layer_rows(part)
     short_count = qry_len.shape[0]
+    own = pack_own(w_qkv, w_o, w_in, w_out, biases, gains, in_bias)
+    rows = own.shape[0]
+    if near:
+        whole = gather(own).reshape(parts, rows, D)
+    else:
+        whole = lax.all_gather(own, "fsdp", axis=0)
+    all_biases, all_gains, all_in_bias = small_parts(
+        whole[:, layers * cuts[4] :], parts, layers, part, hidden_part
+    )
+
+    def unpanel(block):
+        count = block.shape[1] // part
+        return block.reshape(parts, count, part, D).transpose(0, 2, 1, 3).reshape(D, count * D)
+
     inputs = hidden.astype(jnp.float32)
-    layer_inputs = []
-    fetched = []
-    for which_layer in range(layer_count):
-        weights = fetch_layer(w_qkv, w_o, w_in, w_out, biases, gains, in_bias, which_layer)
-        layer_inputs.append(inputs)
-        fetched.append(weights)
-        inputs, unused_kept = layer_forward(inputs, weights, qry_len, psg_len)
+    kept_each, weights_each = [], []
+    for layer in range(layers):
+        block = whole[:, layer * cuts[4] : (layer + 1) * cuts[4]]
+        weights = (
+            unpanel(block[:, cuts[0] : cuts[1]]),
+            unpanel(block[:, cuts[1] : cuts[2]]),
+            unpanel(block[:, cuts[2] : cuts[3]]),
+            block[:, cuts[3] :].reshape(-1, D),
+            all_biases[layer],
+            all_gains[layer],
+            all_in_bias[layer],
+        )
+        inputs, kept = layer_forward(inputs, weights, qry_len, psg_len)
+        kept_each.append(kept)
+        weights_each.append(weights)
     short_live = (jnp.arange(SHORT)[None, :] < qry_len[:, None]).astype(
         jnp.float32
     ) / qry_len.astype(jnp.float32)[:, None]
@@ -234,89 +669,54 @@
     d_inputs = join_kinds(
         short_live[:, :, None] * qry_grad[:, None, :], long_live[:, :, None] * psg_grad[:, None, :]
     )
-    grads_each = [None] * layer_count
-    for which_layer in range(layer_count - 1, -1, -1):
-        weights = fetch_layer(w_qkv, w_o, w_in, w_out, biases, gains, in_bias, which_layer)
-        unused_outputs, kept = layer_forward(layer_inputs[which_layer], weights, qry_len, psg_len)
-        d_inputs, local_grads = layer_backward(d_inputs, weights, kept, short_count)
-        shares = (
-            lax.psum_scatter(local_grads[0], "fsdp", scatter_dimension=0, tiled=True),
-            lax.psum_scatter(local_grads[1], "fsdp", scatter_dimension=0, tiled=True),
-            lax.psum_scatter(local_grads[2], "fsdp", scatter_dimension=0, tiled=True),
-            lax.psum_scatter(local_grads[3], "fsdp", scatter_dimension=0, tiled=True),
-            lax.psum_scatter(local_grads[4], "fsdp", scatter_dimension=1, tiled=True),
-            lax.psum_scatter(local_grads[5], "fsdp", scatter_dimension=1, tiled=True),
-            lax.psum_scatter(local_grads[6], "fsdp", scatter_dimension=0, tiled=True),
+
+    def panel(grad):
+        count = grad.shape[1] // D
+        return grad.reshape(parts, part, count, D).transpose(0, 2, 1, 3).reshape(parts, -1, D)
+
+    grads_each = [None] * layers
+    for layer in range(layers - 1, -1, -1):
+        d_inputs, grads_each[layer] = layer_backward(
+            d_inputs, weights_each[layer], kept_each[layer], short_count
         )
-        parted = (
-            lax.psum_scatter(
-                shares[0].astype(jnp.bfloat16), "rep", scatter_dimension=1, tiled=True
-            ).astype(jnp.float32),
-            lax.psum_scatter(
-                shares[1].astype(jnp.bfloat16), "rep", scatter_dimension=1, tiled=True
-            ).astype(jnp.float32),
-            lax.psum_scatter(
-                shares[2].astype(jnp.bfloat16), "rep", scatter_dimension=1, tiled=True
-            ).astype(jnp.float32),
-            lax.psum_scatter(
-                shares[3].astype(jnp.bfloat16), "rep", scatter_dimension=1, tiled=True
-            ).astype(jnp.float32),
-            lax.psum_scatter(
-                shares[4].astype(jnp.bfloat16), "rep", scatter_dimension=0, tiled=True
-            ).astype(jnp.float32),
-            lax.psum_scatter(
-                shares[5].astype(jnp.bfloat16), "rep", scatter_dimension=0, tiled=True
-            ).astype(jnp.float32),
-            lax.psum_scatter(
-                shares[6].reshape(2, -1).astype(jnp.bfloat16),
-                "rep",
-                scatter_dimension=0,
-                tiled=True,
-            ).astype(jnp.float32),
-        )
-        joined = (
-            lax.all_gather(parted[0].astype(jnp.bfloat16), "rep", axis=1, tiled=True).astype(
-                jnp.float32
-            ),
-            lax.all_gather(parted[1].astype(jnp.bfloat16), "rep", axis=1, tiled=True).astype(
-                jnp.float32
-            ),
-            lax.all_gather(parted[2].astype(jnp.bfloat16), "rep", axis=1, tiled=True).astype(
-                jnp.float32
-            ),
-            lax.all_gather(parted[3].astype(jnp.bfloat16), "rep", axis=1, tiled=True).astype(
-                jnp.float32
-            ),
-            lax.all_gather(parted[4].astype(jnp.bfloat16), "rep", axis=0, tiled=True).astype(
-                jnp.float32
-            ),
-            lax.all_gather(parted[5].astype(jnp.bfloat16), "rep", axis=0, tiled=True).astype(
-                jnp.float32
-            ),
-            lax.all_gather(parted[6].astype(jnp.bfloat16), "rep", axis=0, tiled=True).astype(
-                jnp.float32
-            ),
-        )
-        grads_each[which_layer] = (
-            joined[0],
-            joined[1],
-            joined[2],
-            joined[3],
-            joined[4],
-            joined[5],
-            joined[6].reshape(-1),
-        )
-    totals = tuple((stack_member(grads_each, member) for member in range(7)))
+    pieces = []
+    for grads in grads_each:
+        pieces += [panel(g.astype(jnp.bfloat16)) for g in grads[:3]]
+        pieces.append(grads[3].astype(jnp.bfloat16).reshape(parts, -1, D))
+    small = [
+        jnp.stack([g[which] for g in grads_each])
+        .reshape(layers, -1, parts, size)
+        .transpose(2, 0, 1, 3)
+        .reshape(parts, -1)
+        for which, size in ((4, part), (5, part), (6, hidden_part))
+    ]
+    small = jnp.concatenate(small, axis=1).astype(jnp.bfloat16)
+    small = jnp.pad(small, ((0, 0), (0, (rows - layers * cuts[4]) * D - small.shape[1])))
+    pieces.append(small.reshape(parts, -1, D))
+    partial = jnp.concatenate(pieces, axis=1)
+    if near:
+        total = scatter(partial.reshape(4, 2, 2, rows, D))
+    else:
+        total = lax.psum_scatter(partial.astype(jnp.float32), "fsdp", scatter_dimension=0)
+        total = lax.psum(total, "rep")
+    grads = total[: layers * cuts[4]].reshape(layers, cuts[4], D)
+
+    def unpack(first, last):
+        block = grads[:, first:last].reshape(layers, -1, part, D)
+        return block.transpose(0, 2, 1, 3).reshape(layers, part, -1)
+
+    small = total[layers * cuts[4] :].reshape(1, -1)
+    d_biases, d_gains, d_in_bias = small_parts(small, 1, layers, part, hidden_part)
     return (
         inputs.astype(jnp.bfloat16),
         d_inputs.astype(jnp.bfloat16),
-        totals[0],
-        totals[1],
-        totals[2],
-        totals[3],
-        totals[4],
-        totals[5],
-        totals[6],
+        unpack(cuts[0], cuts[1]),
+        unpack(cuts[1], cuts[2]),
+        unpack(cuts[2], cuts[3]),
+        grads[:, cuts[3] :],
+        d_biases,
+        d_gains,
+        d_in_bias,
     )
 
 
@@ -335,8 +735,10 @@
         P(None, None, "fsdp"),
         P(None, "fsdp"),
     )
+    parts = mesh.shape["fsdp"]
+    near = parts == 16 and mesh.shape["rep"] == 2
     return jax.shard_map(
-        shards,
+        functools.partial(shards, parts=parts, near=near),
         mesh=mesh,
         in_specs=placed,
         out_specs=(

time: 2580 us -> 820 us (0.32)
  waiting for transfers between devices: 1700 us -> 0 us
  blocking collectives: 355 us -> 0 us
  Pallas kernels: 0 us -> 252 us
  local copies, waits for them, and re-layouts: 127 us -> 244 us
  matrix products: 297 us -> 264 us
    reduce_scatter x10 -> x0, waiting for transfers between devices: 811 us -> none  [the longest x2 346 us: shards(): lax.psum_scatter(local_grads[2], 'fsdp', scatter_dimension=0, tiled=True)]
    unnamed x38 -> x0, waiting for transfers between devices: 735 us -> none
    all_gather x20 -> x0, blocking collectives: 278 us -> none  [the longest x2 92.9 us: fetch_layer(): lax.all_gather(gains[which_layer], 'fsdp', axis=1, tiled=True)]
    pallas_call x0 -> x2, Pallas kernels: none -> 252 us  [the longest x1 127 us: gather(): pl.pallas_call(functools.partial(gather_kernel, rows // PAIR), out_shape=...]
    all_gather x8 -> x0, waiting for transfers between devices: 156 us -> none  [the longest x2 78.6 us: fetch_layer(): lax.all_gather(w_in[which_layer], 'fsdp', axis=0, tiled=True)]
    unnamed x2 -> x0, blocking collectives: 77.2 us -> none
    reshape x7 -> x19, local copies, waits for them, and re-layouts: 4.05 us -> 53 us  [the longest x6 44.9 us: panel(): grad.reshape(parts, part, count, D).transpose(0, 2, 1, 3)]
    slice x4 -> x2, local copies, waits for them, and re-layouts: 36.4 us -> 0.37 us  [layer_forward(): outputs = norm_rows(second_resid, gain_float[1], bias_float[5])]
  transfers between devices with their start and end apart: 28 -> 0, of which waited for: 21 -> 0; matrix products, arithmetic and copies ran while one was open for 15% -> 0% of each run, Pallas kernels for 0% -> 0%
where the time goes in v1:
time: 820 us; the launch traced here: 811 us
  matrix products  264 us (32%)
  Pallas kernels  252 us (31%)
  local copies, waits for them, and re-layouts  244 us (30%)
  other arithmetic  47.4 us (6%)
    pallas_call x1, Pallas kernels, gather(): pl.pallas_call(functools.partial(gather_kernel, rows // PAIR), out_shape=...  127 us
    pallas_call x1, Pallas kernels, scatter(): pl.pallas_call(functools.partial(scatter_kernel, rows // PAIR, tuple(shap...  125 us
    unnamed x316, local copies, waits for them, and re-layouts  64.1 us
    dot_general x2, matrix products, layer_forward(): jnp.dot(first_low, w_in, preferred_element_type=jnp.float32)  56.5 us
    reshape x6, local copies, waits for them, and re-layouts, panel(): grad.reshape(parts, part, count, D).transpose(0, 2, 1, 3)  44.9 us
    dot_general x2, matrix products, layer_backward(): d_active = jnp.dot(d_down_low, w_out.T, preferred_element_type=jnp.float32)  25.2 us
    sub x4, matrix products, attend_kind(): exponentials = jnp.exp(scores - highest)  24.5 us
    dot_general x4, matrix products, attend_back(): jnp.einsum('bqhd,bkhd->bhqk', d_context, value_rows, preferred_element_ty...  19.2 us

profile of v1, /device:TPU:0, one launch (start us, length us, event | category | flops | bytes accessed | tf_op | source)
XLA Modules:
  0.0 810.7 jit_solution(18032601940910142252)
XLA Ops:
  8.6 11.0 %multiply_reduce_fusion.16 = f32[768]{0:T(1024)S(1)} fusion(f32[2,128]{1,0:T(2,128)S(1)} %get-tuple-element.114, f32[2,768]{0,1:T(8,128)S(1)} %copy.155), kind=kLoop, calls=%fused_computation.186 | loop fusion | flops 392448 | bytes 10240 | tf_op jit(solution)/shard_map/transpose(jvp())/reduce_sum | solution.py:426
  26.7 126.7 %gather_weights.1 = bf16[4,2,2,1184,768]{4,3,2,1,0:T(8,128)(2,1)} custom-call(bf16[1184,768]{1,0:T(8,128)(2,1)S(1)} %constant_dynamic-update-slice_fusion.own), custom_call_target="tpu_custom_call" | custom-call | tf_op jit(solution)/shard_map/gather_weights/pallas_call | solution.py:187
  163.9 3.2 fusion.153
  167.0 3.5 fusion.152
  170.6 13.0 %fusion.151 = (bf16[16,192,768]{2,1,0:T(8,128)(2,1)}, bf16[16,192,768]{2,1,0:T(8,128)(2,1)S(1)}, bf16[16,192,768]{2,1,0:T(8,128)(2,1)}, bf16[16,192,768]{2,1,0:T(8,128)(2,1)}) fusion(bf16[16,1184,768]{2,1,0:T(8,128)(2,1)} %bitcast.363), kind=kLoop, calls=%fused_computation.338 | loop fusion | bytes 37748736 | tf_op jit(solution)/shard_map/slice | solution.py:655
  183.6 2.4 copy.153
  186.1 3.3 copy.229
  189.4 2.4 copy.136
  192.6 2.4 copy.144
  195.0 2.7 copy.227
  197.8 4.3 fusion.25
  203.3 3.2 reshape.814
  208.4 3.1 fusion.162
  213.8 4.9 copy.143
  218.7 3.2 copy.226
  221.9 7.4 fusion.161
  229.4 5.9 fusion.53
  239.1 28.3 %multiply_convert_fusion.3 = (bf16[768,3072]{1,0:T(8,128)(2,1)S(1)}, f32[768,3072]{1,0:T(8,128)}, f32[768,3072]{1,0:T(8,128)}) fusion(f32[3072]{0:T(1024)S(1)} %copy-done.90, bf16[768,3072]{1,0:T(8,128)(2,1)S(1)} %bitcast.413, f32[768,768]{0,1:T(8,128)S(1)} %get-tuple-element.121, f32[768]{0:T(1024)S(1)} %add.192, f32[768]{0:T(1024)S(1)} %mul.442, ...), kind=kOutput, calls=%fused_computation.33 | convolution fusion | flops 3782541312 | bytes 30695424 | tf_op jit(solution)/shard_map/dot_general | solution.py:515
  267.5 4.4 fusion.164
  272.9 3.5 add_convert_fusion
  278.1 4.3 copy.151
  283.8 3.2 reshape.826
  288.9 3.1 fusion.166
  294.2 10.9 %fusion.165 = (f32[12,512]{1,0:T(8,128)S(1)}, f32[12,512,512]{1,2,0:T(8,128)}) fusion(pred[512]{0:T(512)(128)(4,1)S(1)} %copy-done.108, bf16[1,512,3,12,64]{1,4,3,2,0:T(8,128)(2,1)} %bitcast.392), kind=kOutput, calls=%fused_computation.352 | convolution fusion | flops 415236608 | bytes 14180864 | tf_op jit(solution)/shard_map/sub | solution.py:458
  305.2 6.1 fusion.59
  314.4 28.2 %multiply_convert_fusion.2 = (bf16[768,3072]{1,0:T(8,128)(2,1)S(1)}, f32[768,3072]{1,0:T(8,128)}, f32[768,3072]{1,0:T(8,128)}) fusion(f32[3072]{0:T(1024)S(1)} %copy-done.92, bf16[768,3072]{1,0:T(8,128)(2,1)S(1)} %bitcast.420, f32[768,768]{0,1:T(8,128)S(1)} %get-tuple-element.130, f32[768]{0:T(1024)S(1)} %copy-done.98, f32[768]{0:T(1024)S(1)} %copy-done.74, ...), kind=kOutput, calls=%fused_computation.20 | convolution fusion | flops 3782541312 | bytes 30695424 | tf_op jit(solution)/shard_map/dot_general | solution.py:515
  342.6 2.2 copy-done.111
  344.8 4.6 fusion.168
  353.9 12.7 %fusion.169 = (bf16[3072]{0:T(1024)(128)(2,1)}, bf16[768,3072]{1,0:T(8,128)(2,1)}) fusion(f32[768,3072]{1,0:T(8,128)} %get-tuple-element.78, bf16[3072,768]{1,0:T(8,128)(2,1)S(1)} %bitcast.406, f32[768,768]{0,1:T(8,128)S(1)} %get-tuple-element.76, f32[768]{0:T(1024)S(1)} %negate_multiply_fusion.5, f32[768,3072]{1,0:T(8,128)} %get-tuple-element.131, ...), kind=kOutput, calls=%fused_computation.356 | convolution fusion | flops 3662803968 | bytes 30692352 | tf_op jit(solution)/shard_map/dot_general | solution.py:559
  366.6 8.8 %multiply_reduce_fusion.3 = (bf16[768]{0:T(1024)(128)(2,1)}, f32[768]{0:T(1024)S(1)}, bf16[768]{0:T(1024)(128)(2,1)}, f32[768,768]{0,1:T(8,128)S(1)}) fusion(f32[768,768]{0,1:T(8,128)S(1)} %get-tuple-element.130, f32[768]{0:T(1024)S(1)} %fusion.114, f32[768]{0:T(1024)S(1)} %broadcast_multiply_fusion.2, f32[768]{0:T(1024)S(1)} %copy-done.74, ...), kind=kOutput, calls=%fused_computation.84 | convolution fusion | flops 3629774592 | bytes 16533504 | tf_op jit(solution)/shard_map/dot_general | solution.py:564
  375.4 8.5 %convolution_convert_fusion.2 = bf16[3072,768]{1,0:T(8,128)(2,1)} fusion(bf16[768,3072]{1,0:T(8,128)(2,1)} %copy-done.111, f32[768,768]{0,1:T(8,128)S(1)} %get-tuple-element.76, f32[768]{0:T(1024)S(1)} %negate_multiply_fusion.5), kind=kOutput, calls=%fused_computation.60 | convolution fusion | flops 3627417600 | bytes 11799552 | tf_op jit(solution)/shard_map/dot_general | solution.py:558
  385.3 5.9 convolution_convert_fusion.3
  395.5 9.9 %reshape.842 = bf16[16,48,4,768]{3,2,1,0:T(4,128)(2,1)} reshape(bf16[768,3072]{1,0:T(8,128)(2,1)} %convolution_convert_fusion.3) | data formatting | bytes 9437184 | tf_op jit(solution)/shard_map/reshape | solution.py:675
  405.4 5.3 copy.186
  425.3 2.2 fusion.89
  430.7 7.8 fusion.69
  457.4 6.9 multiply_reduce_fusion.1
  464.3 7.1 multiply_convert_fusion.1
  476.7 5.1 multiply_reduce_fusion.4
  481.8 6.2 convolution_convert_fusion
  488.8 12.5 %fusion.170 = (bf16[3072]{0:T(1024)(128)(2,1)S(1)}, bf16[768,3072]{1,0:T(8,128)(2,1)}) fusion(f32[768,3072]{1,0:T(8,128)} %get-tuple-element.80, bf16[3072,768]{1,0:T(8,128)(2,1)S(1)} %bitcast.402, f32[768,768]{0,1:T(8,128)S(1)} %get-tuple-element.72, f32[768]{0:T(1024)S(1)} %negate_multiply_fusion.3, f32[768,3072]{1,0:T(8,128)} %get-tuple-element.122, ...), kind=kOutput, calls=%fused_computation.357 | convolution fusion | flops 3662803968 | bytes 30692352 | tf_op jit(solution)/shard_map/dot_general | solution.py:559
  501.4 9.7 %multiply_reduce_fusion.5 = (bf16[768]{0:T(1024)(128)(2,1)S(1)}, f32[768]{0:T(1024)S(1)}, bf16[768]{0:T(1024)(128)(2,1)S(1)}, f32[768,768]{0,1:T(8,128)}) fusion(f32[768,768]{0,1:T(8,128)S(1)} %copy-done.2, f32[768]{0:T(1024)S(1)} %copy-done.77, f32[768]{0:T(1024)S(1)} %copy-done.52, f32[768]{0:T(1024)S(1)} %copy-done.71, bf16[768,3072]{1,0:T(8,128)(2,1)} %bitcast.410, ...), kind=kOutput, calls=%fused_computation.86 | convolution fusion | flops 3629774592 | bytes 16533504 | tf_op jit(solution)/shard_map/dot_general | solution.py:564
  511.1 8.0 convolution_convert_fusion.4
  519.4 2.4 fusion.145
  522.4 5.7 convolution_convert_fusion.5
  531.6 9.9 %reshape.840 = bf16[16,48,4,768]{3,2,1,0:T(4,128)(2,1)} reshape(bf16[768,3072]{1,0:T(8,128)(2,1)} %convolution_convert_fusion.5) | data formatting | bytes 9437184 | tf_op jit(solution)/shard_map/reshape | solution.py:675
  541.5 5.6 copy.184
  558.7 7.5 fusion.72
  571.2 2.2 stack.142
  580.4 5.5 reshape.841
  585.9 3.0 copy.185
  589.1 11.3 %multiply_reduce_fusion = (f32[12,512]{1,0:T(8,128)S(1)}, f32[12,512,512]{1,2,0:T(8,128)}) fusion(f32[12,512,512]{1,2,0:T(8,128)} %get-tuple-element.117, f32[12,512]{1,0:T(8,128)S(1)} %copy-done.63, bf16[512,12,64]{0,2,1:T(8,128)(2,1)S(1)} %bitcast.455, bf16[1,512,3,12,64]{1,4,3,2,0:T(8,128)(2,1)S(1)} %bitcast.389), kind=kOutput, calls=%fused_computation.7 | convolution fusion | flops 412084224 | bytes 26796032 | tf_op jit(solution)/shard_map/bqhd,bkhd->bhqk/dot_general | solution.py:474
  601.5 7.0 multiply_convert_fusion
  613.7 5.3 add_convert_fusion.2
  619.0 6.0 fusion.24
  625.0 5.8 copy.182
  630.8 2.4 copy.193
  645.6 8.8 %reshape.839 = bf16[16,48,3,768]{3,2,1,0:T(4,128)(2,1)} reshape(bf16[768,2304]{1,0:T(8,128)(2,1)} %copy.182) | data formatting | bytes 7077888 | tf_op jit(solution)/shard_map/reshape | solution.py:675
  654.4 3.0 copy.183
  660.7 2.6 constant_dynamic-update-slice_fusion.31
  663.3 2.8 constant_dynamic-update-slice_fusion.30
  669.3 2.7 constant_dynamic-update-slice_fusion.27
  672.1 2.6 constant_dynamic-update-slice_fusion.26
  675.6 125.1 %sum_gradients.1 = f32[1184,768]{1,0:T(8,128)S(1)} custom-call(bf16[4,2,2,1184,768]{4,3,2,1,0:T(8,128)(2,1)} %constant_dynamic-update-slice_fusion.25.partial), custom_call_target="tpu_custom_call" | custom-call | tf_op jit(solution)/shard_map/sum_gradients/pallas_call | solution.py:400
  (507 shorter events, 161.6 us)
Async XLA Ops:
  0.6 20.9 %copy-start.38 = (bf16[2,48,2304]{2,1,0:T(8,128)(2,1)S(1)}, bf16[2,48,2304]{2,1,0:T(8,128)(2,1)}, u32[]{:S(2)}) copy-start(bf16[2,48,2304]{2,1,0:T(8,128)(2,1)} %param.17) | copy-start | bytes 1327108
  161.5 149.8 %copy-start.96 = (f32[768]{0:T(1024)}, f32[768]{0:T(1024)S(1)}, u32[]{:S(2)}) copy-start(f32[768]{0:T(1024)S(1)} %add.202) | copy-start | bytes 9220
  161.6 105.8 %copy-start.70 = (f32[768]{0:T(1024)}, f32[768]{0:T(1024)S(1)}, u32[]{:S(2)}) copy-start(f32[768]{0:T(1024)S(1)} %mul.442) | copy-start | bytes 9220
  161.7 149.7 %copy-start.72 = (f32[768]{0:T(1024)}, f32[768]{0:T(1024)S(1)}, u32[]{:S(2)}) copy-start(f32[768]{0:T(1024)S(1)} %mul.451) | copy-start | bytes 9220
  161.8 105.6 %copy-start.94 = (f32[768]{0:T(1024)}, f32[768]{0:T(1024)S(1)}, u32[]{:S(2)}) copy-start(f32[768]{0:T(1024)S(1)} %add.192) | copy-start | bytes 9220
  203.3 26.1 %copy-start.8 = (bf16[512,2304]{0,1:T(8,128)(2,1)}, bf16[512,2304]{0,1:T(8,128)(2,1)S(1)}, u32[]{:S(2)}) copy-start(bf16[512,2304]{0,1:T(8,128)(2,1)S(1)} %slice.394) | copy-start | bytes 7077892
  213.7 21.6 %copy-start.43 = (bf16[96,8,2,128]{3,1,2,0:T(8,128)(2,1)}, bf16[96,8,2,128]{3,1,2,0:T(8,128)(2,1)S(1)}, u32[]{:S(2)}) copy-start(bf16[96,8,2,128]{3,1,2,0:T(8,128)(2,1)S(1)} %copy.297) | copy-start | bytes 1179652
  229.4 6.0 copy-start.61
  229.4 6.0 copy-start.27
  229.4 6.0 copy-start.29
  229.4 6.0 copy-start.102
  235.4 32.0 %slice-start.7 = ((s8[4718592]{0:T(1024)(128)(4,1)}), s8[4194304]{0:T(1024)(128)(4,1)S(1)}, s32[]{:S(2)}) async-start(s8[4718592]{0:T(1024)(128)(4,1)} %bitcast.397), calls=%async_computation.7 | async-start | bytes 8388608
  236.7 30.7 %copy-start.1 = (f32[768,768]{0,1:T(8,128)}, f32[768,768]{0,1:T(8,128)S(1)}, u32[]{:S(2)}) copy-start(f32[768,768]{0,1:T(8,128)S(1)} %get-tuple-element.121) | copy-start | bytes 7077892
  236.8 30.7 %copy-start.51 = (f32[768]{0:T(1024)}, f32[768]{0:T(1024)S(1)}, u32[]{:S(2)}) copy-start(f32[768]{0:T(1024)S(1)} %broadcast_multiply_fusion.4) | copy-start | bytes 9220
  239.1 28.4 %copy-start.76 = (f32[768]{0:T(1024)}, f32[768]{0:T(1024)S(1)}, u32[]{:S(2)}) copy-start(f32[768]{0:T(1024)S(1)} %fusion.112) | copy-start | bytes 9220
  239.1 28.4 %slice-start.8 = ((s8[4718592]{0:T(1024)(128)(4,1)}), s8[524288]{0:T(1024)(128)(4,1)S(1)}, s32[]{:S(2)}) async-start(s8[4718592]{0:T(1024)(128)(4,1)} %bitcast.397), calls=%async_computation.8 | async-start | bytes 1048576
  239.1 28.4 %copy-start.101 = (f32[768]{0:T(1024)S(1)}, f32[768]{0:T(1024)}, u32[]{:S(2)}) copy-start(f32[768]{0:T(1024)} %add.197) | copy-start | bytes 9220
  267.5 5.4 copy-start.14
  271.9 39.4 %copy-start.3 = (f32[768,768]{0,1:T(8,128)}, f32[768,768]{0,1:T(8,128)S(1)}, u32[]{:S(2)}) copy-start(f32[768,768]{0,1:T(8,128)S(1)} %get-tuple-element.124) | copy-start | bytes 7077892
  272.0 39.4 %copy-start.53 = (f32[768]{0:T(1024)}, f32[768]{0:T(1024)S(1)}, u32[]{:S(2)}) copy-start(f32[768]{0:T(1024)S(1)} %broadcast_multiply_fusion.3) | copy-start | bytes 9220
  272.9 38.5 %copy-start.78 = (f32[768]{0:T(1024)}, f32[768]{0:T(1024)S(1)}, u32[]{:S(2)}) copy-start(f32[768]{0:T(1024)S(1)} %fusion.113) | copy-start | bytes 9220
  294.2 17.2 %copy-start.45 = (bf16[96,8,2,128]{3,1,2,0:T(8,128)(2,1)}, bf16[96,8,2,128]{3,1,2,0:T(8,128)(2,1)S(1)}, u32[]{:S(2)}) copy-start(bf16[96,8,2,128]{3,1,2,0:T(8,128)(2,1)S(1)} %copy.296) | copy-start | bytes 1179652
  305.2 6.1 copy-start.64
  305.2 6.2 copy-start.31
  305.2 6.2 copy-start.100
  311.4 33.4 %slice-start.11 = ((s8[4718592]{0:T(1024)(128)(4,1)}), s8[4194304]{0:T(1024)(128)(4,1)S(1)}, s32[]{:S(2)}) async-start(s8[4718592]{0:T(1024)(128)(4,1)} %bitcast.403), calls=%async_computation.11 | async-start | bytes 8388608
  314.4 30.5 %slice-start.12 = ((s8[4718592]{0:T(1024)(128)(4,1)}), s8[524288]{0:T(1024)(128)(4,1)S(1)}, s32[]{:S(2)}) async-start(s8[4718592]{0:T(1024)(128)(4,1)} %bitcast.403), calls=%async_computation.12 | async-start | bytes 1048576
  314.4 30.5 %copy-start.99 = (f32[768]{0:T(1024)S(1)}, f32[768]{0:T(1024)}, u32[]{:S(2)}) copy-start(f32[768]{0:T(1024)} %add.217) | copy-start | bytes 9220
  366.6 18.6 %slice-start.21 = ((s8[4718592]{0:T(1024)(128)(4,1)}), s8[4194304]{0:T(1024)(128)(4,1)S(1)}, s32[]{:S(2)}) async-start(s8[4718592]{0:T(1024)(128)(4,1)} %bitcast.472), calls=%async_computation.21 | async-start | bytes 8388608
  375.4 9.9 %slice-start.22 = ((s8[4718592]{0:T(1024)(128)(4,1)}), s8[524288]{0:T(1024)(128)(4,1)S(1)}, s32[]{:S(2)}) async-start(s8[4718592]{0:T(1024)(128)(4,1)} %bitcast.472), calls=%async_computation.22 | async-start | bytes 1048576
  405.4 5.3 copy-start.81
  410.7 14.6 %copy-start.69 = (f32[2,12,128]{2,1,0:T(8,128)S(1)}, f32[2,12,128]{2,1,0:T(8,128)}, u32[]{:S(2)}) copy-start(f32[2,12,128]{2,1,0:T(8,128)} %copy-done.68) | copy-start | bytes 36868
  430.7 7.8 copy-start.23
  430.7 7.8 copy-start.42
  430.7 7.8 copy-start.47
  457.4 7.0 copy-start.65
  464.3 7.1 copy-start.10
  476.7 12.0 %slice-start.9 = ((s8[4718592]{0:T(1024)(128)(4,1)}), s8[4194304]{0:T(1024)(128)(4,1)S(1)}, s32[]{:S(2)}) async-start(s8[4718592]{0:T(1024)(128)(4,1)} %bitcast.400), calls=%async_computation.9 | async-start | bytes 8388608
  481.8 6.3 copy-start.58
  481.8 6.9 slice-start.10
  488.8 12.6 %copy-start.2 = (f32[768,768]{0,1:T(8,128)S(1)}, f32[768,768]{0,1:T(8,128)}, u32[]{:S(2)}) copy-start(f32[768,768]{0,1:T(8,128)} %copy-done.1) | copy-start | bytes 7077892
  488.8 12.6 %copy-start.52 = (f32[768]{0:T(1024)S(1)}, f32[768]{0:T(1024)}, u32[]{:S(2)}) copy-start(f32[768]{0:T(1024)} %copy-done.51) | copy-start | bytes 9220
  488.8 12.6 %copy-start.71 = (f32[768]{0:T(1024)S(1)}, f32[768]{0:T(1024)}, u32[]{:S(2)}) copy-start(f32[768]{0:T(1024)} %copy-done.70) | copy-start | bytes 9220
  488.8 12.6 %copy-start.77 = (f32[768]{0:T(1024)S(1)}, f32[768]{0:T(1024)}, u32[]{:S(2)}) copy-start(f32[768]{0:T(1024)} %copy-done.76) | copy-start | bytes 9220
  501.4 9.7 %copy-start.56 = (f32[768]{0:T(1024)S(1)}, f32[768]{0:T(1024)}, u32[]{:S(2)}) copy-start(f32[768]{0:T(1024)} %copy-done.55) | copy-start | bytes 9220
  522.4 6.9 copy-start.5
  522.4 5.8 copy-start.30
  541.5 5.6 copy-start.6
  547.1 6.0 copy-start.85
  547.1 6.6 copy-start.86
  547.1 7.2 copy-start.84
  547.1 7.8 copy-start.83
  547.2 9.4 %copy-start.22 = (f32[2,12,128,128]{2,3,1,0:T(8,128)S(1)}, f32[2,12,128,128]{2,3,1,0:T(8,128)}, u32[]{:S(2)}) copy-start(f32[2,12,128,128]{2,3,1,0:T(8,128)} %get-tuple-element.119) | copy-start | bytes 4718596
  547.2 9.4 %copy-start.67 = (f32[2,12,128]{2,1,0:T(8,128)S(1)}, f32[2,12,128]{2,1,0:T(8,128)}, u32[]{:S(2)}) copy-start(f32[2,12,128]{2,1,0:T(8,128)} %copy-done.66) | copy-start | bytes 36868
  558.7 7.5 copy-start.40
  571.2 9.1 %copy-start.16 = (bf16[768,2304]{1,0:T(8,128)(2,1)S(1)}, bf16[768,2304]{1,0:T(8,128)(2,1)}, u32[]{:S(2)}) copy-start(bf16[768,2304]{1,0:T(8,128)(2,1)} %convolution_convert_fusion) | copy-start | bytes 10616836
  588.9 11.6 %slice-start.4 = ((s8[12582912]{0:T(1024)(128)(4,1)}), s8[4194304]{0:T(1024)(128)(4,1)S(1)}, s32[]{:S(2)}) async-start(s8[12582912]{0:T(1024)(128)(4,1)} %bitcast.385), calls=%async_computation.4 | async-start | bytes 8388608
  589.1 11.3 %slice-start.5 = ((s8[12582912]{0:T(1024)(128)(4,1)}), s8[4194304]{0:T(1024)(128)(4,1)S(1)}, s32[]{:S(2)}) async-start(s8[12582912]{0:T(1024)(128)(4,1)} %bitcast.385), calls=%async_computation.5 | async-start | bytes 8388608
  589.1 12.4 %slice-start.6 = ((s8[12582912]{0:T(1024)(128)(4,1)}), s8[4194304]{0:T(1024)(128)(4,1)S(1)}, s32[]{:S(2)}) async-start(s8[12582912]{0:T(1024)(128)(4,1)} %bitcast.385), calls=%async_computation.6 | async-start | bytes 8388608
  613.7 5.3 copy-start.25
  630.8 7.9 copy-start.87
  630.8 11.5 %copy-start.50 = (bf16[16,384]{1,0:T(8,128)(2,1)S(1)}, bf16[16,384]{1,0:T(8,128)(2,1)}, u32[]{:S(2)}) copy-start(bf16[16,384]{1,0:T(8,128)(2,1)} %reshape.845) | copy-start | bytes 36868
  654.4 6.3 slice-start.2
  663.3 6.0 slice-start
  (71 other events, 159.3 us)
